TPU v7x, 256 devices: a whole 4x4x8 slice. The times are simulated.
256 devices in a mesh: pb: 4 (over y_lo, core), ta: 64 (over y_hi, z, x).
Axes of the slice: x: 4, y: 4 (y_hi: 2, y_lo: 2; y = y_hi * 2 + y_lo), z: 8, core: 2. Of those that a mesh axis runs over, the one named last changes fastest.
Arguments:
- source_feats: bfloat16 [128, 512, 128], P('pb', 'ta'), may hold values from -36 to 36, as said below
- target_feats: bfloat16 [128, 65536], P(None, 'ta'), may hold values from -36 to 36, as said below
- back_flow: bfloat16 [2, 65536], P(None, 'ta'), may hold values from -1.1953125 to 1.1953125
- attn_weights: bfloat16 [2, 4, 128, 128], replicated, may hold values from -0.5 to 0.5
- norm_gain: float32 [2, 128], replicated, may hold values from 0.1 to 1.9
- fetch_list: int32 [256, 4], P(('pb', 'ta')), may hold values from 0 to 63
- dest_local: int32 [128, 512], P('pb', 'ta'), may hold values from 0 to 4095
Outputs:
- flow_field: float32 [2, 128, 512], P(None, 'pb', 'ta')
- consistency: float32 [128, 512], P('pb', 'ta')
Inputs may be any that keep to these rules, and one draw needn't show every extreme that they name: `source_feats`: feature values. `target_feats`: feature values.
All inputs are finite; a program needn't handle non-finite values.
Results may differ from a plain program's by a relative error of at most 0.029.
The roundings to bfloat16 on the way count: a program that leaves them out, or rounds other values in their place, can miss the bound.
Values may be sent and summed in bfloat16 or wider, within the bound.
A program may use at most 128 MiB of HBM per device.

v0:
```python
import math

import jax
import jax.numpy as jnp
from jax import lax
from jax.experimental import pallas as pl
from jax.experimental.pallas import tpu as pltpu
from jax.sharding import PartitionSpec as P

MESH = pl.DeviceIdType.MESH
NORM_EPSILON = 1e-05
MATCH_GAIN = 2.0
FLOW_ALPHA = 0.01
FLOW_BETA = 0.5
CH = 128
PB, TA = 4, 64
NX, NZ = 4, 8
FRAME_ROWS, FRAME_COLS = 128, 512
TILE_ROWS, TILE_COLS = 32, 8
PIXELS = TILE_ROWS * TILE_COLS
BLOCKS = NZ
LAST = 2 * BLOCKS - 1
GROUP = 4
ROW_STEP = 2 * GROUP
ORIGINS = ((0, 0), (0, 1), (0, 3), (1, 0), (0, 2), (1, 1), (1, 3), (1, 2))
HOPS = ((0, 1, 0, 1), (0, 2, 0, -1), (0, 3, 1, 0), (2, 4, 0, -1), (1, 5, 1, 0), (2, 6, 1, 0), (3, 7, 0, 2))
CHUNKS, CHUNK_COLS = 8, 64
NEG = -1e30
SCORE_LOG2 = MATCH_GAIN / math.sqrt(CH) * math.log2(math.e)


def tree_sum(xs):
    xs = list(xs)
    while len(xs) > 1:
        xs = [xs[i] + xs[i + 1] for i in range(0, len(xs), 2)]
    return xs[0]


def weighted_tree(xs, weights):
    odd, cur = [], list(xs)
    while len(cur) > 1:
        odd.append(tree_sum(cur[1::2]))
        cur = [cur[i] + cur[i + 1] for i in range(0, len(cur), 2)]
    total = None
    for value, weight in zip(odd, weights):
        term = value * float(weight)
        total = term if total is None else total + term
    return cur[0], total


def normed(message, gain):
    center = message - jnp.mean(message, axis=-1, keepdims=True)
    spread = jnp.mean(center * center, axis=-1, keepdims=True)
    return center * lax.rsqrt(spread + NORM_EPSILON) * gain


def attend(queries, keys, values, admitted):
    scores = lax.dot_general(
        queries, keys, (((1,), (1,)), ((), ())), preferred_element_type=jnp.float32
    ) * (1.0 / math.sqrt(CH))
    scores = jnp.where(admitted, scores, NEG)
    raised = jnp.exp(scores - jnp.max(scores, axis=-1, keepdims=True))
    weights = (raised / jnp.sum(raised, axis=-1, keepdims=True)).astype(jnp.bfloat16)
    return jnp.dot(weights, values, preferred_element_type=jnp.float32).astype(jnp.bfloat16)


def project(pixels, matrix):
    return jnp.dot(pixels, matrix, preferred_element_type=jnp.float32).astype(jnp.bfloat16)


def iota(shape, axis):
    return lax.broadcasted_iota(jnp.int32, shape, axis)


def place():
    pb, ta = lax.axis_index("pb"), lax.axis_index("ta")
    yh, z, x = lax.div(ta, 32), lax.rem(lax.div(ta, NX), NZ), lax.rem(ta, NX)
    return pb, ta, yh, z, x


def kernel(
    src_hbm, tgt_hbm, back_hbm, w_hbm, gain_hbm, fetch_hbm, dest_hbm, flow_ref, cons_ref,
    src_ref, tgt_ref, back_ref, w_ref, gain_ref, fetch_ref, dest_ref, load_sem,
    tset, bset, qset, halo, res, rset, state, first_top, even, odd,
    t_send, t_recv, f_send, f_recv, b_send, b_recv,
    q_send, q_recv, r_send, r_recv, h_send, h_recv,
):
    pb, ta, yh, z, x = place()
    core = lax.rem(pb, 2)
    mate = (pb + 1 - 2 * core, ta)
    up, down = lax.rem(pb + PB - 1, PB), lax.rem(pb + 1, PB)
    left, right = lax.rem(ta + TA - 1, TA), lax.rem(ta + 1, TA)

    def z_peer(offset):
        return (pb, yh * 32 + lax.rem(z + offset + NZ, NZ) * NX + x)

    def x_peer(side, offset):
        far = core + 2 * (1 - lax.div(pb, 2))
        half = yh + side - 2 * yh * side
        return (pb + side * (far - pb), half * 32 + z * NX + lax.rem(x + offset + NX, NX))

    def remote(src, dst, send, recv, device):
        return pltpu.make_async_remote_copy(
            src_ref=src, dst_ref=dst, send_sem=send, recv_sem=recv, device_id=device, device_id_type=MESH
        )

    halo_copies = [
        remote(halo.at[:, 16:32], halo.at[:, 144:160], h_send.at[0], h_recv.at[0], (up, ta)),
        remote(halo.at[:, 128:144], halo.at[:, 0:16], h_send.at[1], h_recv.at[1], (down, ta)),
        remote(halo.at[1, 16:144], halo.at[0, 176:304], h_send.at[2], h_recv.at[2], (pb, right)),
        remote(halo.at[0, 16:144], halo.at[1, 176:304], h_send.at[3], h_recv.at[3], (pb, left)),
        remote(halo.at[1, 16:32], halo.at[0, 304:320], h_send.at[4], h_recv.at[4], (up, right)),
        remote(halo.at[1, 128:144], halo.at[0, 160:176], h_send.at[5], h_recv.at[5], (down, right)),
        remote(halo.at[0, 16:32], halo.at[1, 304:320], h_send.at[6], h_recv.at[6], (up, left)),
        remote(halo.at[0, 128:144], halo.at[1, 160:176], h_send.at[7], h_recv.at[7], (down, left)),
    ]

    loads = [
        pltpu.make_async_copy(a, b, load_sem.at[n])
        for n, (a, b) in enumerate(
            (
                (tgt_hbm, tgt_ref), (back_hbm, back_ref), (src_hbm, src_ref), (w_hbm, w_ref),
                (gain_hbm, gain_ref), (fetch_hbm, fetch_ref), (dest_hbm, dest_ref),
            )
        )
    ]
    for copy in loads:
        copy.start()

    barrier = pltpu.get_barrier_semaphore()
    for device in (
        (up, ta), (down, ta), (pb, right), (pb, left), (up, right), (down, right), (up, left), (down, left), mate,
        x_peer(0, 1), x_peer(0, 2), x_peer(0, 3), x_peer(1, 0),
    ):
        pl.semaphore_signal(barrier, inc=1, device_id=device, device_id_type=MESH)

    def greet(o, carry):
        pl.semaphore_signal(barrier, inc=1, device_id=z_peer(o), device_id_type=MESH)
        return carry

    lax.fori_loop(1, NZ, greet, 0)

    half = pl.ds(core * (CHUNKS // 2), CHUNKS // 2)
    other_half = pl.ds((1 - core) * (CHUNKS // 2), CHUNKS // 2)

    def block_copy(n):
        held, rank, side, steps = HOPS[n]
        return remote(tset.at[held, half], tset.at[rank, half], t_send.at[n], t_recv.at[rank], x_peer(side, steps))

    def back_copy(n):
        held, rank, side, steps = HOPS[n]
        return remote(bset.at[held], bset.at[rank], b_send.at[n], b_recv.at[rank], x_peer(side, steps))

    def mate_copy(rank, part):
        return remote(tset.at[rank, part], tset.at[rank, part], f_send.at[rank], f_recv.at[rank], mate)

    def pass_on(n):
        block_copy(n).start()
        back_copy(n).start()

    def take(n):
        block_copy(n).wait_recv()
        back_copy(n).wait_recv()
        mate_copy(HOPS[n][1], half).start()

    for copy in loads[:2]:
        copy.wait()
    turned = tgt_ref[...].T
    for g in range(CHUNKS):
        for r in range(2):
            at = r * FRAME_COLS + g * CHUNK_COLS
            tset[0, g, r * CHUNK_COLS : (r + 1) * CHUNK_COLS] = turned[at : at + CHUNK_COLS]
    back = back_ref[...].astype(jnp.float32)
    bset[0] = jnp.concatenate([back[:, CH * n : CH * n + CH] for n in range(8)], axis=0).astype(jnp.bfloat16)
    for copy in loads[2:]:
        copy.wait()
    picks = dest_ref[...]
    listed = jnp.zeros_like(picks)
    for n in range(4):
        listed = jnp.where((picks >> 10) == n, fetch_ref[0:1, n : n + 1], listed)
    dests = listed * 1024 + (picks & 1023)
    pixel = iota((TILE_ROWS, PIXELS), 1)
    row_of = ((pixel >> 2) & 31) == iota((TILE_ROWS, PIXELS), 0)
    row_hot = jnp.where(row_of, 1.0, 0.0).astype(jnp.bfloat16)
    pixel = iota((TILE_COLS, PIXELS), 1)
    col_of = (pixel >> 7) * 4 + (pixel & 3) == iota((TILE_COLS, PIXELS), 0)
    spread = [
        jnp.dot(part.astype(jnp.float32).astype(jnp.bfloat16), row_hot, preferred_element_type=jnp.float32)
        for part in (dests >> 8, dests & 255)
    ]
    spread = jnp.where(col_of, spread[0] * 256.0 + spread[1], 0.0)
    spread = jnp.sum(spread, axis=0, keepdims=True)
    coarse = jnp.floor(spread * (1.0 / 256.0))
    pair = jnp.concatenate([coarse, spread - coarse * 256.0], axis=0)
    qset[0, PIXELS:] = jnp.concatenate(
        [pair[:, :CH], pair[:, CH:], jnp.zeros((12, CH), jnp.float32)], axis=0
    ).astype(jnp.bfloat16)

    i = iota((PIXELS, PIXELS), 0)
    j = iota((PIXELS, PIXELS), 1)
    wanted = ((i >> 2) & 31) * 8 + (i >> 7) * 4 + (i & 3)
    order = jnp.where(wanted == j, 1.0, 0.0).astype(jnp.bfloat16)
    pixels = project(order, src_ref[...])
    same = ((i >> 5) & 3) == ((j >> 5) & 3)
    attended = attend(
        project(pixels, w_ref[0, 0]), project(pixels, w_ref[0, 1]), project(pixels, w_ref[0, 2]), same
    )
    message = jnp.dot(attended, w_ref[0, 3], preferred_element_type=jnp.float32)
    one = (pixels.astype(jnp.float32) + normed(message, gain_ref[0:1])).astype(jnp.bfloat16)
    halo[0, 16:144] = one[:128]
    halo[1, 16:144] = one[128:]
    pl.semaphore_wait(barrier, 13 + (BLOCKS - 1))
    for copy in halo_copies:
        copy.start()
    for n in (0, 1, 2):
        pass_on(n)
    for copy in halo_copies:
        copy.wait()

    i = iota((128, 320), 0)
    j = iota((128, 320), 1)
    beside = j >= 160
    kk = jnp.where(beside, j - 160, j)
    row, key_row = i >> 2, (kk >> 2) - 4
    low = pb * TILE_ROWS + row < 4
    key_low = ((pb * TILE_ROWS + key_row + FRAME_ROWS) & (FRAME_ROWS - 1)) < 4
    rows_agree = (((row + 4) >> 3) == (kk >> 5)) & (low == key_low)
    for h, edge in ((0, 0), (1, TA - 1)):
        admitted = rows_agree & jnp.logical_not(beside & (ta == edge))
        around = halo[h]
        own = halo[h, 16:144]
        attended = attend(
            project(own, w_ref[1, 0]), project(around, w_ref[1, 1]), project(around, w_ref[1, 2]), admitted
        )
        message = jnp.dot(attended, w_ref[1, 3], preferred_element_type=jnp.float32)
        two = (own.astype(jnp.float32) + normed(message, gain_ref[1:2])).astype(jnp.bfloat16)
        qset[0, h * 128 : (h + 1) * 128] = (two.astype(jnp.float32) * SCORE_LOG2).astype(jnp.bfloat16)

    def nth(k):
        odd = lax.rem(k, 2)
        return lax.rem(odd * lax.div(k + 1, 2) + (1 - odd) * (NZ - lax.div(k, 2)), NZ)

    def query_copy(o):
        held = jnp.where((o == 3), 2, jnp.where((o == 4) | (o == 5), 6, 0))
        return remote(qset.at[held], qset.at[o], q_send.at[o], q_recv.at[o], z_peer(lax.rem(o - held + NZ, NZ)))

    def result_copy(o):
        return remote(res.at[o], rset.at[o], r_send.at[o], r_recv.at[o], z_peer(-o))

    query_copy(1).start()
    query_copy(7).start()
    query_copy(2).start()
    query_copy(6).start()
    take(0)
    pass_on(4)
    take(1)
    pass_on(3)
    pass_on(5)
    take(2)
    pass_on(6)
    for rank in (1, 2, 3):
        mate_copy(rank, other_half).wait_recv()

    sub = iota((8, PIXELS), 0).astype(jnp.float32)
    origins = [(yh + side - 2 * yh * side, lax.rem(x + NX - o, NX)) for side, o in ORIGINS]
    base = (z * 8).astype(jnp.float32)
    row_weights = [(half_of * 64 + column * 2).astype(jnp.float32) for half_of, column in origins]

    def score_chunk(g, late, queries, buffer, top):
        feats = tset[pl.ds(late * GROUP, GROUP), g].reshape(ROW_STEP * CHUNK_COLS, CH)
        scores = lax.dot_general(
            feats, queries, (((1,), (1,)), ((), ())), preferred_element_type=jnp.float32
        )
        buffer[...] = scores
        return jnp.maximum(top, jnp.max(scores.reshape(-1, 8, PIXELS), axis=0))

    def sum_chunk(g, weights, buffer, top, new_top, sums):
        s0, s1, s2 = sums
        fade = jnp.exp2(top - new_top)
        scores = buffer[...].reshape(ROW_STEP, CHUNK_COLS // 8, 8, PIXELS)
        raised = jnp.exp2(scores - new_top[None, None])
        by_row = jnp.sum(raised, axis=1)
        by_col = jnp.sum(raised, axis=0)
        total, col_part = weighted_tree([by_col[n] for n in range(CHUNK_COLS // 8)], (8, 16, 32))
        row_part = tree_sum([by_row[2 * n + 1] for n in range(GROUP)]) + total * base
        for n in range(GROUP):
            row_part = row_part + (by_row[2 * n] + by_row[2 * n + 1]) * weights[n]
        col_part = col_part + total * (sub + float(g * CHUNK_COLS))
        return s0 * fade + row_part, s1 * fade + col_part, s2 * fade + total

    state[0] = jnp.zeros((4, 8, PIXELS), jnp.float32)
    res[0] = jnp.zeros((8, PIXELS), jnp.float32)
    floor = jnp.full((8, PIXELS), NEG, jnp.float32)
    buffers = (even, odd)

    def item(step):
        first, second, last = step < 5, step < 9, step == LAST
        late = jnp.where(first, 0, jnp.where(second | last, 1, lax.rem(step + 1, 2)))
        k = jnp.where(first, step, jnp.where(second, step - 4, jnp.where(last, 0, lax.div(step + 1, 2))))
        return late, nth(k)

    def finish_block(o, late):
        top, s0, s1, s2 = tuple(state[o, m] for m in range(4))
        best = jnp.max(top, axis=0, keepdims=True)
        scale = jnp.exp2(top - best)
        t0 = jnp.sum(s0 * scale, axis=0, keepdims=True)
        t1 = jnp.sum(s1 * scale, axis=0, keepdims=True)
        t2 = jnp.sum(s2 * scale, axis=0, keepdims=True)

        marks = qset[o, PIXELS:].astype(jnp.float32)
        dest = jnp.concatenate(
            [marks[0:1] * 256.0 + marks[1:2], marks[2:3] * 256.0 + marks[3:4]], axis=1
        ).astype(jnp.int32)
        block, off = dest >> 10, dest & 1023
        here = ((block >> 2) & 7) == z
        at = jnp.zeros_like(block)
        for rank, (half_of, column) in enumerate(origins):
            at = jnp.where((block >> 5 == half_of) & ((block & 3) == column), rank * 16, at)
        at = jnp.where(here, at + (off >> 7) * 2, -1000) - late * (GROUP * 16)
        lanes = jnp.where(iota((CH, PIXELS), 0) == (off & 127), 1.0, 0.0).astype(jnp.bfloat16)
        table = bset[pl.ds(late * GROUP, GROUP)].reshape(GROUP * 16, CH)
        picked = jnp.dot(table, lanes, preferred_element_type=jnp.float32)
        line = iota((GROUP * 16, PIXELS), 0)
        back0 = jnp.sum(jnp.where(line == at, picked, 0.0), axis=0, keepdims=True)
        back1 = jnp.sum(jnp.where(line == at + 1, picked, 0.0), axis=0, keepdims=True)
        known = jnp.where(late == 1, res[o, 4:6], 0.0)
        back0, back1 = back0 + known[0:1], back1 + known[1:2]
        pad = jnp.zeros((2, PIXELS), jnp.float32)
        res[o] = jnp.concatenate([best, t0, t1, t2, back0, back1, pad], axis=0)

    def match_step(step, carry):
        late, o = item(step)
        before_late, before_o = item(jnp.where(step == LAST, 0, jnp.maximum(step - 1, 0)))
        alone = (step == 0) | (step == 4) | (step == LAST)
        next_late, next_o = item(jnp.where(alone, step, step + 1))

        @pl.when(step == 1)
        def _():
            query_copy(o).wait_recv()

        @pl.when((next_late == 0) & jnp.logical_not(alone))
        def _():
            query_copy(next_o).wait_recv()

        @pl.when(step == 2)
        def _():
            query_copy(3).start()

        @pl.when(step == 3)
        def _():
            query_copy(5).start()
            query_copy(4).start()

        @pl.when(step == 4)
        def _():
            for hop in (3, 4, 5, 6):
                take(hop)

        @pl.when(step == 5)
        def _():
            for rank in range(GROUP, BLOCKS):
                mate_copy(rank, other_half).wait_recv()

        queries, next_queries = qset[o, :PIXELS], qset[next_o, :PIXELS]

        @pl.when((step == 0) | (step == 1) | (step == 5))
        def _():
            first_top[...] = score_chunk(0, late, queries, even, floor)

        @pl.when(step == LAST)
        def _():
            done_late, done_o = item(LAST - 1)
            finish_block(done_o, done_late)
            result_copy(done_o).start()

        next_top = first_top[...]
        finish_block(before_o, before_late)
        weights = [jnp.where(late == 1, b, a) for a, b in zip(row_weights[:GROUP], row_weights[GROUP:])]
        top = jnp.where(late == 1, state[o, 0], floor)
        sums = tuple(jnp.where(late == 1, state[o, m], 0.0) for m in range(1, 4))
        next_top = jnp.maximum(next_top, top)
        for g in range(CHUNKS):
            last, top = top, next_top
            if g + 1 < CHUNKS:
                next_top = score_chunk(g + 1, late, queries, buffers[(g + 1) % 2], top)
            else:
                next_top = score_chunk(0, next_late, next_queries, even, floor)
            sums = sum_chunk(g, weights, buffers[g % 2], last, top, sums)
        state[o, 0] = top
        for m in range(3):
            state[o, m + 1] = sums[m]

        first_top[...] = next_top

        @pl.when((step > 0) & (before_late == 1) & (before_o > 0))
        def _():
            result_copy(before_o).start()

        return carry

    lax.fori_loop(0, 2 * BLOCKS, match_step, 0)
    finish_block(0, 1)

    def settle(n, carry):
        remote(res.at[n], rset.at[n], r_send.at[n], r_recv.at[n], mate).wait_recv()
        return carry

    lax.fori_loop(1, BLOCKS, settle, 0)
    parts = [res[0]] + [rset[n] for n in range(1, BLOCKS)]
    best = parts[0]
    for part in parts[1:]:
        best = jnp.maximum(best, part)
    best = best[0:1]
    total = jnp.zeros((8, PIXELS), jnp.float32)
    back = jnp.zeros((8, PIXELS), jnp.float32)
    for part in parts:
        total = total + part * jnp.exp2(part[0:1] - best)
        back = back + part
    p = iota((1, PIXELS), 1)
    row = (pb * TILE_ROWS + ((p >> 2) & 31)).astype(jnp.float32) / FRAME_ROWS
    col = (ta * TILE_COLS + (p >> 7) * 4 + (p & 3)).astype(jnp.float32) / FRAME_COLS
    flow0 = total[1:2] / total[3:4] / FRAME_ROWS - row
    flow1 = total[2:3] / total[3:4] / FRAME_COLS - col
    back0, back1 = back[4:5], back[5:6]
    diff = (flow0 + back0) ** 2 + (flow1 + back1) ** 2
    mag = flow0**2 + flow1**2 + back0**2 + back1**2
    cons = jnp.exp(-diff / (FLOW_ALPHA * mag + FLOW_BETA))
    moved = []
    for value in (flow0, flow1, cons):
        for _ in range(3):
            part = value.astype(jnp.bfloat16).astype(jnp.float32)
            moved.append(jnp.where(col_of, part, 0.0))
            value = value - part
    moved = lax.dot_general(
        jnp.concatenate(moved, axis=0).astype(jnp.bfloat16), row_hot, (((1,), (1,)), ((), ())),
        preferred_element_type=jnp.float32,
    )
    moved = [moved[n * TILE_COLS : (n + 1) * TILE_COLS] for n in range(9)]
    flow_ref[0] = moved[0] + moved[1] + moved[2]
    flow_ref[1] = moved[3] + moved[4] + moved[5]
    cons_ref[...] = moved[6] + moved[7] + moved[8]

    for n in range(NZ - 1):
        block_copy(n).wait_send()
        back_copy(n).wait_send()
        mate_copy(n + 1, half).wait_send()

    def finish(o, carry):
        query_copy(o).wait_send()
        result_copy(o).wait_send()
        return carry

    lax.fori_loop(1, BLOCKS, finish, 0)


def shards(source_feats, target_feats, back_flow, attn_weights, norm_gain, fetch_list, dest_local):
    vmem = pl.BlockSpec(memory_space=pltpu.VMEM)

    def dma(count):
        return pltpu.SemaphoreType.DMA((count,))

    args = (
        source_feats.reshape(PIXELS, CH), target_feats, back_flow, attn_weights, norm_gain, fetch_list, dest_local.T,
    )
    flow, cons = pl.pallas_call(
        kernel,
        out_shape=(
            pltpu.VMEM((2, TILE_COLS, TILE_ROWS), jnp.float32),
            pltpu.VMEM((TILE_COLS, TILE_ROWS), jnp.float32),
        ),
        in_specs=[pl.BlockSpec(memory_space=pl.ANY)] * len(args),
        out_specs=(vmem, vmem),
        scratch_shapes=[pltpu.VMEM(a.shape, a.dtype) for a in args]
        + [dma(len(args))]
        + [
            pltpu.VMEM((NZ, CHUNKS, 2 * CHUNK_COLS, CH), jnp.bfloat16),
            pltpu.VMEM((NZ, 16, CH), jnp.bfloat16),
            pltpu.VMEM((NZ, PIXELS + 16, CH), jnp.bfloat16),
            pltpu.VMEM((2, 320, CH), jnp.bfloat16),
            pltpu.VMEM((BLOCKS, 8, PIXELS), jnp.float32),
            pltpu.VMEM((BLOCKS, 8, PIXELS), jnp.float32),
            pltpu.VMEM((BLOCKS, 4, 8, PIXELS), jnp.float32),
            pltpu.VMEM((8, PIXELS), jnp.float32),
            pltpu.VMEM((ROW_STEP * CHUNK_COLS, PIXELS), jnp.float32),
            pltpu.VMEM((ROW_STEP * CHUNK_COLS, PIXELS), jnp.float32),
        ]
        + [dma(8)] * 12,
        compiler_params=pltpu.CompilerParams(
            collective_id=0, has_side_effects=True, vmem_limit_bytes=60 << 20
        ),
    )(*args)
    return jnp.swapaxes(flow, 1, 2), cons.T


def solution(mesh):
    placed = (
        P("pb", "ta", None),
        P(None, "ta"),
        P(None, "ta"),
        P(),
        P(),
        P(("pb", "ta"), None),
        P("pb", "ta"),
    )
    return jax.shard_map(
        shards,
        mesh=mesh,
        in_specs=placed,
        out_specs=(P(None, "pb", "ta"), P("pb", "ta")),
        check_vma=False,
    )
```

profile of v0, /device:TPU:1, one launch (start us, length us, event | category | flops | bytes accessed | tf_op | source)
XLA Modules:
  0.0 47.5 jit_solution(4435921767503618423)
XLA Ops:
  0.6 45.7 %shard_map.86 = (f32[2,8,32]{2,1,0:T(8,128)S(1)}, f32[8,32]{1,0:T(8,128)S(1)}) custom-call(bf16[256,128]{1,0:T(8,128)(2,1)} %bitcast.6, bf16[128,1024]{1,0:T(8,128)(2,1)} %tgt_hbm.1, bf16[2,1024]{1,0:T(2,128)(2,1)} %back_hbm.1, bf16[2,4,128,128]{3,2,1,0:T(8,128)(2,1)} %w_hbm.1, f32[2,128]{1,0:T(2,128)} %gain_hbm.1, s32[1,4]{1,0:T(1,128)} %fetch_hbm.1, ...), custom_call_target="tpu_custom_call" | custom-call | tf_op jit(solution)/shard_map/pallas_call | solution.py:465
  46.3 0.6 %copy.11 = f32[2,32,8]{1,2,0:T(8,128)} copy(f32[2,32,8]{1,2,0:T(8,128)S(1)} %bitcast.4) | data formatting | bytes 4096
  46.9 0.6 %copy.12 = f32[32,8]{0,1:T(8,128)} copy(f32[32,8]{0,1:T(8,128)S(1)} %bitcast.5) | data formatting | bytes 2048
where the time goes:
time: 47.6 us; the launch traced here: 47.5 us
  Pallas kernels  45.7 us (96%)
  local copies, waits for them, and re-layouts  1.19 us (2%)
  between operations  0.64 us (1%)
    pallas_call x1, Pallas kernels, shards(): pl.pallas_call(kernel, out_shape=(pltpu.VMEM((2, TILE_COLS, TILE_ROWS), j...  45.7 us
    unnamed x2, local copies, waits for them, and re-layouts  1.19 us

commit v1 on v0

--- a/solution.py
+++ b/solution.py
@@ -214,8 +214,6 @@
         copy.start()
     for n in (0, 1, 2):
         pass_on(n)
-    for copy in halo_copies:
-        copy.wait()
 
     i = iota((128, 320), 0)
     j = iota((128, 320), 1)
@@ -225,12 +223,15 @@
     low = pb * TILE_ROWS + row < 4
     key_low = ((pb * TILE_ROWS + key_row + FRAME_ROWS) & (FRAME_ROWS - 1)) < 4
     rows_agree = (((row + 4) >> 3) == (kk >> 5)) & (low == key_low)
-    for h, edge in ((0, 0), (1, TA - 1)):
-        admitted = rows_agree & jnp.logical_not(beside & (ta == edge))
+    admitted = [rows_agree & jnp.logical_not(beside & (ta == edge)) for edge in (0, TA - 1)]
+    own_queries = [project(one[h * 128 : (h + 1) * 128], w_ref[1, 0]) for h in range(2)]
+    for copy in halo_copies:
+        copy.wait()
+    for h in range(2):
         around = halo[h]
         own = halo[h, 16:144]
         attended = attend(
-            project(own, w_ref[1, 0]), project(around, w_ref[1, 1]), project(around, w_ref[1, 2]), admitted
+            own_queries[h], project(around, w_ref[1, 1]), project(around, w_ref[1, 2]), admitted[h]
         )
         message = jnp.dot(attended, w_ref[1, 3], preferred_element_type=jnp.float32)
         two = (own.astype(jnp.float32) + normed(message, gain_ref[1:2])).astype(jnp.bfloat16)
@@ -400,6 +401,18 @@
 
     lax.fori_loop(0, 2 * BLOCKS, match_step, 0)
     finish_block(0, 1)
+
+    for n in range(NZ - 1):
+        block_copy(n).wait_send()
+        back_copy(n).wait_send()
+        mate_copy(n + 1, half).wait_send()
+
+    def finish(o, carry):
+        query_copy(o).wait_send()
+        result_copy(o).wait_send()
+        return carry
+
+    lax.fori_loop(1, BLOCKS, finish, 0)
 
     def settle(n, carry):
         remote(res.at[n], rset.at[n], r_send.at[n], r_recv.at[n], mate).wait_recv()
@@ -440,18 +453,6 @@
     flow_ref[1] = moved[3] + moved[4] + moved[5]
     cons_ref[...] = moved[6] + moved[7] + moved[8]
 
-    for n in range(NZ - 1):
-        block_copy(n).wait_send()
-        back_copy(n).wait_send()
-        mate_copy(n + 1, half).wait_send()
-
-    def finish(o, carry):
-        query_copy(o).wait_send()
-        result_copy(o).wait_send()
-        return carry
-
-    lax.fori_loop(1, BLOCKS, finish, 0)
-
 
 def shards(source_feats, target_feats, back_flow, attn_weights, norm_gain, fetch_list, dest_local):
     vmem = pl.BlockSpec(memory_space=pltpu.VMEM)

time: 47.6 us -> 47.4 us (level)
  no operation moved by 1% of the time
where the time goes in v1:
time: 47.4 us; the launch traced here: 47.3 us
  Pallas kernels  45.4 us (96%)
  local copies, waits for them, and re-layouts  1.19 us (3%)
  between operations  0.64 us (1%)
    pallas_call x1, Pallas kernels, shards(): pl.pallas_call(kernel, out_shape=(pltpu.VMEM((2, TILE_COLS, TILE_ROWS), j...  45.4 us
    unnamed x2, local copies, waits for them, and re-layouts  1.19 us

profile of v1, /device:TPU:1, one launch (start us, length us, event | category | flops | bytes accessed | tf_op | source)
XLA Modules:
  0.0 47.3 jit_solution(3209614934206866868)
XLA Ops:
  0.6 45.4 %shard_map.86 = (f32[2,8,32]{2,1,0:T(8,128)S(1)}, f32[8,32]{1,0:T(8,128)S(1)}) custom-call(bf16[256,128]{1,0:T(8,128)(2,1)} %bitcast.6, bf16[128,1024]{1,0:T(8,128)(2,1)} %tgt_hbm.1, bf16[2,1024]{1,0:T(2,128)(2,1)} %back_hbm.1, bf16[2,4,128,128]{3,2,1,0:T(8,128)(2,1)} %w_hbm.1, f32[2,128]{1,0:T(2,128)} %gain_hbm.1, s32[1,4]{1,0:T(1,128)} %fetch_hbm.1, ...), custom_call_target="tpu_custom_call" | custom-call | tf_op jit(solution)/shard_map/pallas_call | solution.py:466
  46.1 0.6 %copy.11 = f32[2,32,8]{1,2,0:T(8,128)} copy(f32[2,32,8]{1,2,0:T(8,128)S(1)} %bitcast.4) | data formatting | bytes 4096
  46.7 0.6 %copy.12 = f32[32,8]{0,1:T(8,128)} copy(f32[32,8]{0,1:T(8,128)S(1)} %bitcast.5) | data formatting | bytes 2048
